TPU v7x, 512 devices: a whole 4x8x8 slice. The times are simulated.
512 devices in a mesh: band: 128 (over z, y_lo, x, core), head: 4 (over y_hi).
Axes of the slice: x: 4, y: 8 (y_hi: 4, y_lo: 2; y = y_hi * 2 + y_lo), z: 8, core: 2. Of those that a mesh axis runs over, the one named last changes fastest.
Arguments:
- queries: bfloat16 [16384, 1536], P('band', 'head'), as said below
- keys: bfloat16 [16384, 1536], P('band', 'head'), as said below
- values: bfloat16 [16384, 1536], P('band', 'head'), may hold values from -6 to 6
- d_out: bfloat16 [16384, 1536], P('band', 'head'), may hold values from -6 to 6
- gain: float32 [1536], P('head'), may hold values from 0.1 to 1.9
- blocks_on: int32 [128, 4], P('band'), may hold values 0 or 1
Outputs:
- out: bfloat16 [16384, 1536], P('band', 'head')
- d_queries: bfloat16 [16384, 1536], P('band', 'head')
- d_keys: bfloat16 [16384, 1536], P('band', 'head')
- d_values: bfloat16 [16384, 1536], P('band', 'head')
Inputs may be any that keep to these rules, and one draw needn't show every extreme that they name: `queries`: entries lie within -180 to 180. `keys`: entries lie within -6 to 6.
All inputs are finite; a program needn't handle non-finite values. No bound on the sum of `blocks_on` on one device may be relied on, other than what follows from the above.
Results may differ from a plain program's by a relative error of at most 0.0063.
Values may be sent and summed in bfloat16 or wider, within the bound.
A program may use at most 64 MiB of HBM per device.

v0:
```python
import jax
import jax.numpy as jnp
from jax import lax
from jax.sharding import PartitionSpec as P

HEAD_DIM = 128


NEG = -1e30
EPS = 1e-06


def from_behind(array, axis, by):
    devices = lax.axis_size(axis)
    pairs = [(i, i + by) for i in range(devices) if 0 <= i + by < devices]
    return lax.ppermute(array, axis, pairs)


def row_pairs_matrix(left, right):
    return lax.dot_general(
        left, right, (((1,), (1,)), ((), ())), preferred_element_type=jnp.float32
    )


def cols_by_cols(left, right):
    return lax.dot_general(
        left, right, (((0,), (0,)), ((), ())), preferred_element_type=jnp.float32
    )


def product(left, right):
    return jnp.dot(left, right, preferred_element_type=jnp.float32)


def one_head(matrix, head_index):
    return matrix[:, head_index * HEAD_DIM : (head_index + 1) * HEAD_DIM]


def local(queries, keys, values, d_out, gain, blocks_on):
    row_count = queries.shape[0]
    heads_here = queries.shape[1] // HEAD_DIM
    blocks = lax.axis_size("band")
    spacing = blocks // 8
    block_offsets = [-2 * spacing, -spacing, spacing, 2 * spacing]
    position = lax.axis_index("band")
    scaling = HEAD_DIM ** (-0.5)
    full_width = queries.shape[1] * lax.axis_size("head")
    key_value = jnp.stack([keys, values])
    reached = [key_value]
    allowed = [jnp.ones((), jnp.bool_)]
    for slot_index, offset in enumerate(block_offsets):
        reached.append(from_behind(key_value, "band", -offset))
        target = position + offset
        allowed.append((target >= 0) & (target < blocks) & (blocks_on[0, slot_index] == 1))
    gathered = jnp.concatenate(reached, axis=1)
    key_all = gathered[0]
    value_all = gathered[1]
    column_ok = jnp.repeat(jnp.stack(allowed), row_count)

    def scores(head_index):
        raw_score = (
            row_pairs_matrix(one_head(queries, head_index), one_head(key_all, head_index)) * scaling
        )
        return jnp.where(column_ok[None, :], raw_score, NEG)

    peaks, totals, pieces = ([], [], [])
    for head_index in range(heads_here):
        score = scores(head_index)
        peak = jnp.max(score, axis=1)
        exponent = jnp.exp(score - peak[:, None])
        total = jnp.sum(exponent, axis=1)
        weight_probs = (exponent / total[:, None]).astype(jnp.bfloat16)
        pieces.append(product(weight_probs, one_head(value_all, head_index)).astype(jnp.bfloat16))
        peaks.append(peak)
        totals.append(total)
    attention = jnp.concatenate(pieces, axis=1)
    attention_wide = attention.astype(jnp.float32)
    square_sum = lax.psum(jnp.sum(attention_wide * attention_wide, axis=1), "head")
    inverse = lax.rsqrt(square_sum / full_width + EPS)
    out = (attention_wide * inverse[:, None] * gain).astype(jnp.bfloat16)
    gradient_pass = d_out.astype(jnp.float32) * gain
    along = lax.psum(jnp.sum(gradient_pass * attention_wide, axis=1), "head")
    d_attn = (
        inverse[:, None] * gradient_pass
        - attention_wide * (inverse**3 * along / full_width)[:, None]
    ).astype(jnp.bfloat16)
    deltas = [
        jnp.sum(
            one_head(d_attn, head_index).astype(jnp.float32) * one_head(attention_wide, head_index),
            axis=1,
        )
        for head_index in range(heads_here)
    ]
    query_parts, key_parts, value_parts = ([], [], [])
    for head_index in range(heads_here):
        score = scores(head_index)
        probs = jnp.exp(score - peaks[head_index][:, None]) / totals[head_index][:, None]
        upstream = one_head(d_attn, head_index)
        d_weights = row_pairs_matrix(upstream, one_head(value_all, head_index))
        d_score = (probs * (d_weights - deltas[head_index][:, None])).astype(jnp.bfloat16)
        query_parts.append(product(d_score, one_head(key_all, head_index)) * scaling)
        weight_probs = probs.astype(jnp.bfloat16)
        key_parts.append(cols_by_cols(d_score, one_head(queries, head_index)) * scaling)
        value_parts.append(cols_by_cols(weight_probs, upstream))
    d_queries = jnp.concatenate(query_parts, axis=1).astype(jnp.bfloat16)
    stacked_grads = jnp.stack(
        [jnp.concatenate(key_parts, axis=1), jnp.concatenate(value_parts, axis=1)]
    )
    summed = stacked_grads[:, :row_count]
    for slot_index, offset in enumerate(block_offsets):
        outgoing = stacked_grads[
            :, (slot_index + 1) * row_count : (slot_index + 2) * row_count
        ].astype(jnp.bfloat16)
        arrived = from_behind(outgoing, "band", offset)
        summed = summed + arrived.astype(jnp.float32)
    d_keys = summed[0].astype(jnp.bfloat16)
    d_values = summed[1].astype(jnp.bfloat16)
    return (out, d_queries, d_keys, d_values)


def solution(mesh):
    in_specs = (
        P("band", "head"),
        P("band", "head"),
        P("band", "head"),
        P("band", "head"),
        P("head"),
        P("band", None),
    )
    out_specs = (P("band", "head"), P("band", "head"), P("band", "head"), P("band", "head"))
    return jax.shard_map(local, mesh=mesh, in_specs=in_specs, out_specs=out_specs, check_vma=False)
```

profile of v0, /device:TPU:6, one launch (start us, length us, event | category | flops | bytes accessed | tf_op | source)
XLA Modules:
  0.0 70.1 jit_solution(15155738258795446889)
XLA Ops:
  0.6 1.0 %pad_maximum_fusion.1 = (bf16[2,128,384]{2,1,0:T(8,128)(2,1)S(1)}, bf16[2,640,384]{2,1,0:T(8,128)(2,1)S(1)}) fusion(bf16[1,128,384]{2,1,0:T(8,128)(2,1)} %bitcast.45, bf16[1,128,384]{2,1,0:T(8,128)(2,1)} %bitcast.46), kind=kLoop, calls=%fused_computation.53 | loop fusion | flops 393215 | bytes 589824 | tf_op jit(solution)/shard_map/stack | solution.py:48
  1.6 1.3 %collective-permute-start.2 = (bf16[2,128,384]{2,1,0:T(8,128)(2,1)S(1)}, bf16[2,128,384]{2,1,0:T(8,128)(2,1)S(1)}, u32[]{:S(2)}, u32[]{:S(2)}) collective-permute-start(bf16[2,128,384]{2,1,0:T(8,128)(2,1)S(1)} %get-tuple-element.23), channel_id=1, source_target_pairs={{64,0},{68,4},{72,8},{76,12},{80,16},{84,20},{88,24},{92,28},{96,3... | collective-permute-start | bytes 589832 | tf_op jit(solution)/shard_map/ppermute | solution.py:16
  2.9 4.9 %collective-permute-start.1 = (bf16[2,128,384]{2,1,0:T(8,128)(2,1)S(1)}, bf16[2,128,384]{2,1,0:T(8,128)(2,1)S(1)}, u32[]{:S(2)}, u32[]{:S(2)}) collective-permute-start(bf16[2,128,384]{2,1,0:T(8,128)(2,1)S(1)} %get-tuple-element.23), channel_id=1, source_target_pairs={{0,64},{4,68},{8,72},{12,76},{16,80},{20,84},{24,88},{28,92},{32,9... | collective-permute-start | bytes 589832 | tf_op jit(solution)/shard_map/ppermute | solution.py:16
  7.8 6.1 %collective-permute-start = (bf16[2,128,384]{2,1,0:T(8,128)(2,1)S(1)}, bf16[2,128,384]{2,1,0:T(8,128)(2,1)S(1)}, u32[]{:S(2)}, u32[]{:S(2)}) collective-permute-start(bf16[2,128,384]{2,1,0:T(8,128)(2,1)S(1)} %get-tuple-element.23), channel_id=1, source_target_pairs={{0,128},{4,132},{8,136},{12,140},{16,144},{20,148},{24,152},{28,15... | collective-permute-start | bytes 589832 | tf_op jit(solution)/shard_map/ppermute | solution.py:16
  13.9 1.3 %collective-permute-start.3 = (bf16[2,128,384]{2,1,0:T(8,128)(2,1)S(1)}, bf16[2,128,384]{2,1,0:T(8,128)(2,1)S(1)}, u32[]{:S(2)}, u32[]{:S(2)}) collective-permute-start(bf16[2,128,384]{2,1,0:T(8,128)(2,1)S(1)} %get-tuple-element.23), channel_id=1, source_target_pairs={{128,0},{132,4},{136,8},{140,12},{144,16},{148,20},{152,24},{156,2... | collective-permute-start | bytes 589832 | tf_op jit(solution)/shard_map/ppermute | solution.py:16
  15.2 1.4 %fusion.59 = (s32[1,1]{1,0:T(1,128)}, s32[1,1]{1,0:T(1,128)}, s32[1,1]{1,0:T(1,128)}, s32[1,1]{1,0:T(1,128)}) fusion(s32[1,4]{1,0:T(1,128)} %param.11), kind=kLoop, calls=%fused_computation.108 | loop fusion | bytes 32 | tf_op jit(solution)/shard_map/slice | solution.py:54
  19.5 1.0 %copy.10 = bf16[128,384]{0,1:T(8,128)(2,1)S(1)} copy(bf16[128,384]{1,0:T(8,128)(2,1)} %param.9) | data formatting | bytes 196608 | tf_op args[3]
  20.6 8.5 %collective-permute-done.3 = bf16[2,128,384]{2,1,0:T(8,128)(2,1)S(1)} collective-permute-done((bf16[2,128,384]{2,1,0:T(8,128)(2,1)S(1)}, bf16[2,128,384]{2,1,0:T(8,128)(2,1)S(1)}, u32[]{:S(2)}, u32[]{:S(2)}) %collective-permute-start.3) | collective-permute-done | bytes 196640 | tf_op jit(solution)/shard_map/ppermute | solution.py:16
  29.3 0.8 %copy-done = bf16[128,384]{1,0:T(8,128)(2,1)S(1)} copy-done((bf16[128,384]{1,0:T(8,128)(2,1)S(1)}, bf16[128,384]{1,0:T(8,128)(2,1)}, u32[]{:S(2)}) %copy-start) | copy-done | bytes 98328
  30.3 0.3 fusion.61
  32.4 12.9 %all-reduce = (f32[128]{0:T(128)S(1)}, f32[128]{0:T(128)S(1)}) all-reduce(f32[128]{0:T(128)S(1)} %get-tuple-element.12, f32[128]{0:T(128)S(1)} %get-tuple-element.11), channel_id=1, replica_groups=mesh['band'=128,'head'=4] {'head'}, use_global_device_ids=true, to_apply=%region_7.8 | all-reduce | flops 256 | bytes 2048 | tf_op jit(solution)/shard_map/psum | solution.py:78
  45.7 0.3 fusion.11
  46.3 0.3 fusion.10
  48.1 0.8 %fusion.58 = (bf16[2,128,384]{2,1,0:T(8,128)(2,1)}, bf16[2,128,384]{2,1,0:T(8,128)(2,1)}, bf16[2,128,384]{2,1,0:T(8,128)(2,1)S(1)}, bf16[2,128,384]{2,1,0:T(8,128)(2,1)S(1)}) fusion(bf16[2,640,384]{2,1,0:T(8,128)(2,1)S(1)} %fusion), kind=kLoop, calls=%fused_computation.107 | loop fusion | bytes 1572864 | tf_op jit(solution)/shard_map/slice | solution.py:111
  48.9 1.3 %collective-permute-start.4 = (bf16[2,128,384]{2,1,0:T(8,128)(2,1)}, bf16[2,128,384]{2,1,0:T(8,128)(2,1)S(1)}, u32[]{:S(2)}, u32[]{:S(2)}) collective-permute-start(bf16[2,128,384]{2,1,0:T(8,128)(2,1)} %get-tuple-element.15), channel_id=1, source_target_pairs={{128,0},{132,4},{136,8},{140,12},{144,16},{148,20},{152,24},{156,2... | collective-permute-start | bytes 589832 | tf_op jit(solution)/shard_map/ppermute | solution.py:16
  50.2 5.5 %collective-permute-start.7 = (bf16[2,128,384]{2,1,0:T(8,128)(2,1)}, bf16[2,128,384]{2,1,0:T(8,128)(2,1)S(1)}, u32[]{:S(2)}, u32[]{:S(2)}) collective-permute-start(bf16[2,128,384]{2,1,0:T(8,128)(2,1)} %get-tuple-element.16), channel_id=1, source_target_pairs={{0,128},{4,132},{8,136},{12,140},{16,144},{20,148},{24,152},{28,15... | collective-permute-start | bytes 589832 | tf_op jit(solution)/shard_map/ppermute | solution.py:16
  55.7 5.0 %collective-permute-start.6 = (bf16[2,128,384]{2,1,0:T(8,128)(2,1)S(1)}, bf16[2,128,384]{2,1,0:T(8,128)(2,1)}, u32[]{:S(2)}, u32[]{:S(2)}) collective-permute-start(bf16[2,128,384]{2,1,0:T(8,128)(2,1)S(1)} %get-tuple-element.17), channel_id=1, source_target_pairs={{0,64},{4,68},{8,72},{12,76},{16,80},{20,84},{24,88},{28,92},{32,9... | collective-permute-start | bytes 589832 | tf_op jit(solution)/shard_map/ppermute | solution.py:16
  60.6 1.3 %collective-permute-start.5 = (bf16[2,128,384]{2,1,0:T(8,128)(2,1)S(1)}, bf16[2,128,384]{2,1,0:T(8,128)(2,1)}, u32[]{:S(2)}, u32[]{:S(2)}) collective-permute-start(bf16[2,128,384]{2,1,0:T(8,128)(2,1)S(1)} %get-tuple-element.18), channel_id=1, source_target_pairs={{64,0},{68,4},{72,8},{76,12},{80,16},{84,20},{88,24},{92,28},{96,3... | collective-permute-start | bytes 589832 | tf_op jit(solution)/shard_map/ppermute | solution.py:16
  61.9 0.3 fusion.12
  62.2 0.8 %copy.20 = bf16[128,384]{1,0:T(8,128)(2,1)} copy(bf16[128,384]{0,1:T(8,128)(2,1)S(1)} %get-tuple-element.26) | data formatting | bytes 196608
  63.0 0.8 %copy.21 = bf16[128,384]{1,0:T(8,128)(2,1)} copy(bf16[128,384]{0,1:T(8,128)(2,1)S(1)} %pad_maximum_fusion.3) | data formatting | bytes 196608
  63.7 4.6 %collective-permute-done.5 = bf16[2,128,384]{2,1,0:T(8,128)(2,1)} collective-permute-done((bf16[2,128,384]{2,1,0:T(8,128)(2,1)S(1)}, bf16[2,128,384]{2,1,0:T(8,128)(2,1)}, u32[]{:S(2)}, u32[]{:S(2)}) %collective-permute-start.5) | collective-permute-done | bytes 196640 | tf_op jit(solution)/shard_map/ppermute | solution.py:16
  68.3 1.1 %fusion.18 = bf16[2,128,384]{2,1,0:T(8,128)(2,1)S(1)} fusion(f32[1,640,384]{2,1,0:T(8,128)S(1)} %get-tuple-element.39, f32[1,640,384]{2,1,0:T(8,128)S(1)} %get-tuple-element.40, bf16[2,128,384]{2,1,0:T(8,128)(2,1)S(1)} %collective-permute-done.7, bf16[2,128,384]{2,1,0:T(8,128)(2,1)} %collective-permute-done.6, ...), kind=kLoop, calls=%fused_computation.40 | loop fusion | flops 983040 | bytes 2949120 | tf_op jit(solution)/shard_map/convert.1
  69.4 0.7 slice_bitcast_fusion.2
  (44 shorter events, 4.6 us)
Async XLA Ops:
  1.6 19.0 %collective-permute-start.2 = (bf16[2,128,384]{2,1,0:T(8,128)(2,1)S(1)}, bf16[2,128,384]{2,1,0:T(8,128)(2,1)S(1)}, u32[]{:S(2)}, u32[]{:S(2)}) collective-permute-start(bf16[2,128,384]{2,1,0:T(8,128)(2,1)S(1)} %get-tuple-element.23), channel_id=1, source_target_pairs={{64,0},{68,4},{72,8},{76,12},{80,16},{84,20},{88,24},{92,28},{96,3... | collective-permute-start | bytes 589832 | tf_op jit(solution)/shard_map/ppermute | solution.py:16
  2.9 17.6 %collective-permute-start.1 = (bf16[2,128,384]{2,1,0:T(8,128)(2,1)S(1)}, bf16[2,128,384]{2,1,0:T(8,128)(2,1)S(1)}, u32[]{:S(2)}, u32[]{:S(2)}) collective-permute-start(bf16[2,128,384]{2,1,0:T(8,128)(2,1)S(1)} %get-tuple-element.23), channel_id=1, source_target_pairs={{0,64},{4,68},{8,72},{12,76},{16,80},{20,84},{24,88},{28,92},{32,9... | collective-permute-start | bytes 589832 | tf_op jit(solution)/shard_map/ppermute | solution.py:16
  7.8 12.6 %collective-permute-start = (bf16[2,128,384]{2,1,0:T(8,128)(2,1)S(1)}, bf16[2,128,384]{2,1,0:T(8,128)(2,1)S(1)}, u32[]{:S(2)}, u32[]{:S(2)}) collective-permute-start(bf16[2,128,384]{2,1,0:T(8,128)(2,1)S(1)} %get-tuple-element.23), channel_id=1, source_target_pairs={{0,128},{4,132},{8,136},{12,140},{16,144},{20,148},{24,152},{28,15... | collective-permute-start | bytes 589832 | tf_op jit(solution)/shard_map/ppermute | solution.py:16
  13.9 15.2 %collective-permute-start.3 = (bf16[2,128,384]{2,1,0:T(8,128)(2,1)S(1)}, bf16[2,128,384]{2,1,0:T(8,128)(2,1)S(1)}, u32[]{:S(2)}, u32[]{:S(2)}) collective-permute-start(bf16[2,128,384]{2,1,0:T(8,128)(2,1)S(1)} %get-tuple-element.23), channel_id=1, source_target_pairs={{128,0},{132,4},{136,8},{140,12},{144,16},{148,20},{152,24},{156,2... | collective-permute-start | bytes 589832 | tf_op jit(solution)/shard_map/ppermute | solution.py:16
  29.2 0.9 %copy-start = (bf16[128,384]{1,0:T(8,128)(2,1)S(1)}, bf16[128,384]{1,0:T(8,128)(2,1)}, u32[]{:S(2)}) copy-start(bf16[128,384]{1,0:T(8,128)(2,1)} %param.6) | copy-start | bytes 294916
  31.5 0.8 %copy-start.1 = (f32[384]{0:T(512)S(1)}, f32[384]{0:T(512)}, u32[]{:S(2)}) copy-start(f32[384]{0:T(512)} %param.10) | copy-start | bytes 4612
  48.9 14.8 %collective-permute-start.4 = (bf16[2,128,384]{2,1,0:T(8,128)(2,1)}, bf16[2,128,384]{2,1,0:T(8,128)(2,1)S(1)}, u32[]{:S(2)}, u32[]{:S(2)}) collective-permute-start(bf16[2,128,384]{2,1,0:T(8,128)(2,1)} %get-tuple-element.15), channel_id=1, source_target_pairs={{128,0},{132,4},{136,8},{140,12},{144,16},{148,20},{152,24},{156,2... | collective-permute-start | bytes 589832 | tf_op jit(solution)/shard_map/ppermute | solution.py:16
  50.2 13.5 %collective-permute-start.7 = (bf16[2,128,384]{2,1,0:T(8,128)(2,1)}, bf16[2,128,384]{2,1,0:T(8,128)(2,1)S(1)}, u32[]{:S(2)}, u32[]{:S(2)}) collective-permute-start(bf16[2,128,384]{2,1,0:T(8,128)(2,1)} %get-tuple-element.16), channel_id=1, source_target_pairs={{0,128},{4,132},{8,136},{12,140},{16,144},{20,148},{24,152},{28,15... | collective-permute-start | bytes 589832 | tf_op jit(solution)/shard_map/ppermute | solution.py:16
  55.7 8.0 %collective-permute-start.6 = (bf16[2,128,384]{2,1,0:T(8,128)(2,1)S(1)}, bf16[2,128,384]{2,1,0:T(8,128)(2,1)}, u32[]{:S(2)}, u32[]{:S(2)}) collective-permute-start(bf16[2,128,384]{2,1,0:T(8,128)(2,1)S(1)} %get-tuple-element.17), channel_id=1, source_target_pairs={{0,64},{4,68},{8,72},{12,76},{16,80},{20,84},{24,88},{28,92},{32,9... | collective-permute-start | bytes 589832 | tf_op jit(solution)/shard_map/ppermute | solution.py:16
  60.6 7.7 %collective-permute-start.5 = (bf16[2,128,384]{2,1,0:T(8,128)(2,1)S(1)}, bf16[2,128,384]{2,1,0:T(8,128)(2,1)}, u32[]{:S(2)}, u32[]{:S(2)}) collective-permute-start(bf16[2,128,384]{2,1,0:T(8,128)(2,1)S(1)} %get-tuple-element.18), channel_id=1, source_target_pairs={{64,0},{68,4},{72,8},{76,12},{80,16},{84,20},{88,24},{92,28},{96,3... | collective-permute-start | bytes 589832 | tf_op jit(solution)/shard_map/ppermute | solution.py:16
where the time goes:
time: 70.6 us; the launch traced here: 70.1 us
  starting transfers between devices  26.6 us (38%)
  waiting for transfers between devices  13.1 us (19%)
  blocking collectives  12.9 us (18%)
  local copies, waits for them, and re-layouts  6.63 us (9%)
  matrix products  4.15 us (6%)
  between operations  3.56 us (5%)
  other arithmetic  3.26 us (5%)
    ppermute x8, starting transfers between devices, from_behind(): return lax.ppermute(array, axis, pairs)  26.6 us
    ppermute x8, waiting for transfers between devices, from_behind(): return lax.ppermute(array, axis, pairs)  13.1 us
    psum x1, blocking collectives, local(): lax.psum(jnp.sum(attention_wide * attention_wide, axis=1), 'head')  12.9 us
    unnamed x10, local copies, waits for them, and re-layouts  3.4 us
    dot_general x6, matrix products, product(): return jnp.dot(left, right, preferred_element_type=jnp.float32)  1.61 us
  transfers between devices with their start and end apart: 8, of which 2 were waited for; matrix products, arithmetic and copies ran while one was open for 6% of the time, Pallas kernels for 0%

commit v1 on v0

v1 whole, which is shorter than its diff:
```python
import functools

import jax
import jax.numpy as jnp
from jax import lax
from jax.experimental import pallas as pl
from jax.experimental.pallas import tpu as pltpu
from jax.sharding import PartitionSpec as P

D = 128
NEG = -1e30
EPS = 1e-06
VMEM = 32 * 1024 * 1024
MESH = pl.DeviceIdType.MESH
BF16 = jnp.bfloat16
F32 = jnp.float32

SLOT_OFFSET = (0, -1, 1, -2, 2)
COLUMN = {-2: 0, -1: 1, 1: 2, 2: 3}
NEAR = {1: 1, -1: 2}
FAR = {1: 3, -1: 4}


def nt(left, right):
    return lax.dot_general(left, right, (((1,), (1,)), ((), ())), preferred_element_type=F32)


def nn(left, right):
    return jnp.dot(left, right, preferred_element_type=F32)


def kernel(
    heads,
    spacing,
    steps,
    peers,
    q_hbm,
    k_hbm,
    v_hbm,
    do_hbm,
    gain_hbm,
    on_hbm,
    out_ref,
    dq_ref,
    dk_ref,
    dv_ref,
    kb,
    vb,
    qb,
    ab,
    dob,
    gain_ref,
    on_ref,
    attn,
    score,
    probs,
    score_t,
    probs_t,
    dk_acc,
    dv_acc,
    st1,
    st2,
    sums,
    send_sem,
    recv_sem,
    local_sem,
):
    me = lax.axis_index("band")
    hd = lax.axis_index("head")
    z = me // spacing
    width = heads * D
    full_width = width * peers
    scaling = D ** (-0.5)

    def inside(offset):
        return (z + offset >= 0) & (z + offset < steps)

    def slot(index):
        return pl.ds(index * D, D)

    def cols(h):
        return slice(h * D, (h + 1) * D)

    barrier = pltpu.get_barrier_semaphore()
    expected = jnp.int32(peers - 1)
    for d in (1, -1):

        @pl.when(inside(d))
        def _():
            pl.semaphore_signal(barrier, 1, device_id=(me + d * spacing, hd), device_id_type=MESH)

        expected = expected + inside(d).astype(jnp.int32)
    for p in range(1, peers):
        pl.semaphore_signal(barrier, 1, device_id=(me, lax.rem(hd + p, peers)), device_id_type=MESH)
    local = []

    def fetch(src, dst):
        copy = pltpu.make_async_copy(src, dst, local_sem.at[len(local)])
        copy.start()
        local.append(copy)

    fetch(on_hbm, on_ref)
    for h in range(heads):
        fetch(q_hbm.at[:, cols(h)], qb.at[h, slot(0)])
        fetch(k_hbm.at[:, cols(h)], kb.at[h, slot(0)])
    for h in range(heads):
        fetch(v_hbm.at[:, cols(h)], vb.at[h, slot(0)])
    fetch(gain_hbm, gain_ref)
    for h in range(heads):
        fetch(do_hbm.at[:, cols(h)], dob.at[h])

    pl.semaphore_wait(barrier, expected)

    used = [0]
    sent = []

    def remote(src, dst, device, condition):
        index = used[0]
        used[0] += 1
        copy = pltpu.make_async_remote_copy(
            src, dst, send_sem.at[index], recv_sem.at[index], device_id=device, device_id_type=MESH
        )
        sent.append((copy, condition))
        return copy

    def first_step(src, dst_of, d):
        copy = remote(src, dst_of(NEAR[d]), (me + d * spacing, hd), inside(d))
        pl.when(inside(d))(copy.start)
        return copy

    def second_step(first, dst_of, d):
        copy = remote(dst_of(NEAR[d]), dst_of(FAR[d]), (me + d * spacing, hd), inside(d) & inside(-d))

        @pl.when(inside(-d))
        def _():
            first.wait_recv()
            pl.when(inside(d))(copy.start)

        return copy

    def arrived(second, d):
        pl.when(inside(-2 * d))(second.wait_recv)

    def rows_of(buffer, h):
        return lambda index: buffer.at[h, slot(index)]

    def tile_of(buffer):
        return lambda index: buffer.at[index]

    both = (1, -1)
    k1 = {(h, d): first_step(k_hbm.at[:, cols(h)], rows_of(kb, h), d) for h in range(heads) for d in both}
    v1 = {(h, d): first_step(v_hbm.at[:, cols(h)], rows_of(vb, h), d) for h in range(heads) for d in both}

    for d in both:
        for index, away in ((NEAR[d], -d), (FAR[d], -2 * d)):

            @pl.when(jnp.logical_not(inside(away)))
            def _():
                for buffer in (kb, vb, qb, ab):
                    for h in range(heads):
                        buffer[h, slot(index)] = jnp.zeros((D, D), BF16)
                st1[index] = jnp.zeros(st1.shape[1:], F32)
                st2[index] = jnp.zeros(st2.shape[1:], F32)

    for copy in local:
        copy.wait()
    allowed = {}
    for offset, column in COLUMN.items():
        allowed[offset] = inside(offset) & (on_ref[0, column] == 1)
    factor = {0: scaling}
    shift = {0: 0.0}
    for offset in COLUMN:
        factor[offset] = jnp.where(allowed[offset], scaling, 0.0).astype(F32)
        shift[offset] = jnp.where(allowed[offset], 0.0, NEG).astype(F32)


    def compute_scores(h, index):
        offset = SLOT_OFFSET[index]
        raw = nt(qb[h, slot(0)], kb[h, slot(index)])
        score[h, :, slot(index)] = raw * factor[offset] + shift[offset]

    for h in range(heads):
        compute_scores(h, 0)
    k2 = {}
    for h in range(heads):
        for d in both:
            k2[h, d] = second_step(k1[h, d], rows_of(kb, h), d)
        for d in both:
            compute_scores(h, NEAR[d])
    v2 = {}
    for h in range(heads):
        for d in both:
            v2[h, d] = second_step(v1[h, d], rows_of(vb, h), d)
    q1 = {(h, d): first_step(q_hbm.at[:, cols(h)], rows_of(qb, h), d) for h in range(heads) for d in both}

    lane = lax.broadcasted_iota(jnp.int32, (D, D), 1)

    def as_rows(columns):
        packed = jnp.zeros((D, D), F32)
        for i, column in enumerate(columns):
            packed = jnp.where(lane == i, column, packed)
        return packed.T

    peaks, inverses = [], []
    for h in range(heads):
        for d in both:
            arrived(k2[h, d], d)
        for d in both:
            compute_scores(h, FAR[d])
        pieces = [score[h, :, slot(i)] for i in range(5)]
        top = functools.reduce(jnp.maximum, pieces)
        peak = jnp.max(top, axis=1, keepdims=True)
        exponents = [jnp.exp(piece - peak) for piece in pieces]
        total = jnp.sum(functools.reduce(jnp.add, exponents), axis=1, keepdims=True)
        inverse_total = 1.0 / total
        for i in range(5):
            weight = exponents[i] * inverse_total
            score[h, :, slot(i)] = weight
            probs[h, :, slot(i)] = weight.astype(BF16)
        peaks.append(peak)
        inverses.append(inverse_total)
    st1[0] = as_rows(peaks + inverses + [-shift[offset] for offset in COLUMN])[0:16]
    s1 = {d: first_step(st1.at[0], tile_of(st1), d) for d in both}

    near_rows = 3 * D
    partial = [nn(probs[h, :, 0:near_rows], vb[h, 0:near_rows]) for h in range(heads)]
    sums_g, sums_a = [], []
    for h in range(heads):
        for d in both:
            arrived(v2[h, d], d)
        value = partial[h] + nn(probs[h, :, near_rows:], vb[h, near_rows:])
        attn[h] = value.astype(BF16)
        wide = attn[h].astype(F32)
        gradient = dob[h].astype(F32) * gain_ref[cols(h)][None, :]
        sums_g.append(jnp.sum(gradient * wide, axis=1, keepdims=True))
        sums_a.append(jnp.sum(wide * wide, axis=1, keepdims=True))
    sums[0] = as_rows([functools.reduce(jnp.add, sums_g), functools.reduce(jnp.add, sums_a)])[0:8]
    exchanged = []
    for p in range(1, peers):
        copy = remote(sums.at[0], sums.at[p], (me, lax.rem(hd + p, peers)), True)
        copy.start()
        exchanged.append(copy)

    s2 = {d: second_step(s1[d], tile_of(st1), d) for d in both}
    q2 = {}
    for h in range(heads):
        for d in both:
            q2[h, d] = second_step(q1[h, d], rows_of(qb, h), d)

    def weights_back(h, index):
        offset = SLOT_OFFSET[index]
        peak = st1[index, h : h + 1]
        if offset:
            row = 2 * heads + COLUMN[-offset]
            peak = peak + st1[index, row : row + 1]
        raw = nt(kb[h, slot(0)], qb[h, slot(index)]) * scaling
        weight = jnp.exp(raw - peak) * st1[index, heads + h : heads + h + 1]
        score_t[h, :, slot(index)] = weight
        probs_t[h, :, slot(index)] = weight.astype(BF16)

    for h in range(heads):
        for index in range(3):
            weights_back(h, index)

    for copy in exchanged:
        copy.wait_recv()
    all_rows = functools.reduce(jnp.add, [sums[p] for p in range(peers)])
    along = all_rows[0:1]
    square = all_rows[1:2]
    inverse = lax.rsqrt(square / full_width + EPS)
    coefficient = inverse * inverse * inverse * along / full_width
    sublane = lax.broadcasted_iota(jnp.int32, (D, D), 0)
    columns = jnp.where(sublane == 0, inverse, coefficient).T
    inverse_col = columns[:, 0:1]
    coefficient_col = columns[:, 1:2]
    a1 = {}
    for h in range(heads):
        gradient = dob[h].astype(F32) * gain_ref[cols(h)][None, :]
        wide = attn[h].astype(F32)
        ab[h, slot(0)] = (inverse_col * gradient - wide * coefficient_col).astype(BF16)
        for d in both:
            a1[h, d] = first_step(ab.at[h, slot(0)], rows_of(ab, h), d)
    deltas = [
        jnp.sum(ab[h, slot(0)].astype(F32) * attn[h].astype(F32), axis=1, keepdims=True) for h in range(heads)
    ]
    st2[0] = as_rows(deltas)[0:8]
    e1 = {d: first_step(st2.at[0], tile_of(st2), d) for d in both}
    for h in range(heads):
        out_ref[:, cols(h)] = (attn[h].astype(F32) * inverse_col * gain_ref[cols(h)][None, :]).astype(BF16)

    def query_gradient(h):
        d_weights = nt(ab[h, slot(0)], vb[h])
        d_score = (score[h] * (d_weights - deltas[h])).astype(BF16)
        dq_ref[:, cols(h)] = (nn(d_score, kb[h]) * scaling).astype(BF16)

    def key_gradients(h, low, high):
        rows = slice(low * D, high * D)
        delta = jnp.concatenate([st2[i, h : h + 1] for i in range(low, high)], axis=1)
        value_part = nn(probs_t[h, :, rows], ab[h, rows])
        d_weights = nt(vb[h, slot(0)], ab[h, rows])
        d_score = (score_t[h, :, rows] * (d_weights - delta)).astype(BF16)
        return nn(d_score, qb[h, rows]), value_part

    for h in range(heads):
        query_gradient(h)
    for h in range(heads):
        dk_acc[h], dv_acc[h] = key_gradients(h, 0, 1)
    for d in both:
        arrived(s2[d], d)
    for h in range(heads):
        for d in both:
            arrived(q2[h, d], d)
        for d in both:
            weights_back(h, FAR[d])
    e2 = {d: second_step(e1[d], tile_of(st2), d) for d in both}
    a2 = {}
    for h in range(heads):
        for d in both:
            a2[h, d] = second_step(a1[h, d], rows_of(ab, h), d)
    for h in range(heads):
        key_part, value_part = key_gradients(h, 1, 3)
        dk_acc[h] += key_part
        dv_acc[h] += value_part
    for d in both:
        arrived(e2[d], d)
    for h in range(heads):
        for d in both:
            arrived(a2[h, d], d)
        key_part, value_part = key_gradients(h, 3, 5)
        dk_ref[:, cols(h)] = ((dk_acc[h] + key_part) * scaling).astype(BF16)
        dv_ref[:, cols(h)] = (dv_acc[h] + value_part).astype(BF16)
    for copy, condition in sent:
        if condition is True:
            copy.wait_send()
        else:
            pl.when(condition)(copy.wait_send)


def hand_on(*refs):
    *refs, sem = refs
    copies = []
    for i, (src, dst) in enumerate(zip(refs[: len(refs) // 2], refs[len(refs) // 2 :])):
        copies.append(pltpu.make_async_copy(src, dst, sem.at[i]))
        copies[-1].start()
    for copy in copies:
        copy.wait()


def local(queries, keys, values, d_out, gain, blocks_on):
    rows, width = queries.shape
    heads = width // D
    spacing = lax.axis_size("band") // 8
    peers = lax.axis_size("head")
    block = jax.ShapeDtypeStruct((rows, width), BF16)
    anywhere = pl.BlockSpec(memory_space=pl.ANY)
    vmem = pl.BlockSpec(memory_space=pltpu.VMEM)
    copies = 2 * 2 * 4 * heads + 8 + peers - 1
    results = pl.pallas_call(
        functools.partial(kernel, heads, spacing, 8, peers),
        out_shape=[block] * 4,
        in_specs=[anywhere] * 6,
        out_specs=[vmem] * 4,
        scratch_shapes=[pltpu.VMEM((heads, 5 * D, D), BF16)] * 4
        + [
            pltpu.VMEM((heads, D, D), BF16),
            pltpu.VMEM((width,), F32),
            pltpu.SMEM((1, 4), jnp.int32),
            pltpu.VMEM((heads, D, D), BF16),
            pltpu.VMEM((heads, D, 5 * D), F32),
            pltpu.VMEM((heads, D, 5 * D), BF16),
            pltpu.VMEM((heads, D, 5 * D), F32),
            pltpu.VMEM((heads, D, 5 * D), BF16),
            pltpu.VMEM((heads, D, D), F32),
            pltpu.VMEM((heads, D, D), F32),
            pltpu.VMEM((5, 16, D), F32),
            pltpu.VMEM((5, 8, D), F32),
            pltpu.VMEM((peers, 8, D), F32),
            pltpu.SemaphoreType.DMA((copies,)),
            pltpu.SemaphoreType.DMA((copies,)),
            pltpu.SemaphoreType.DMA((4 * heads + 2,)),
        ],
        compiler_params=pltpu.CompilerParams(
            collective_id=0, has_side_effects=True, vmem_limit_bytes=VMEM
        ),
        cost_estimate=pl.CostEstimate(flops=505_000_000, bytes_accessed=800_000, transcendentals=500_000),
        name="attention",
    )(*[pltpu.with_memory_space_constraint(x, pltpu.HBM) for x in (queries, keys, values, d_out, gain, blocks_on)])
    passed = pl.pallas_call(
        hand_on,
        out_shape=[block] * 4,
        in_specs=[vmem] * 4,
        out_specs=[anywhere] * 4,
        scratch_shapes=[pltpu.SemaphoreType.DMA((4,))],
        compiler_params=pltpu.CompilerParams(vmem_limit_bytes=8 * 1024 * 1024),
        name="hand_on",
    )(*results)
    return tuple(passed)


def solution(mesh):
    in_specs = (
        P("band", "head"),
        P("band", "head"),
        P("band", "head"),
        P("band", "head"),
        P("head"),
        P("band", None),
    )
    out_specs = (P("band", "head"), P("band", "head"), P("band", "head"), P("band", "head"))
    return jax.shard_map(local, mesh=mesh, in_specs=in_specs, out_specs=out_specs, check_vma=False)
```

time: 70.6 us -> 38.7 us (0.55)
  Pallas kernels: 0 us -> 37.8 us
  starting transfers between devices: 26.6 us -> 0 us
  waiting for transfers between devices: 13.1 us -> 0 us
  blocking collectives: 12.9 us -> 0 us
  local copies, waits for them, and re-layouts: 6.63 us -> 0 us
  matrix products: 4.15 us -> 0 us
  other arithmetic: 3.26 us -> 0 us
  between operations: 3.56 us -> 0.64 us
    pallas_call x0 -> x2, Pallas kernels: none -> 37.8 us  [the longest x1 37 us: local(): pl.pallas_call(functools.partial(kernel, heads, spacing, 8, peers), out_s...]
    ppermute x8 -> x0, starting transfers between devices: 26.6 us -> none  [from_behind(): return lax.ppermute(array, axis, pairs)]
    ppermute x8 -> x0, waiting for transfers between devices: 13.1 us -> none  [from_behind(): return lax.ppermute(array, axis, pairs)]
    psum x1 -> x0, blocking collectives: 12.9 us -> none  [local(): lax.psum(jnp.sum(attention_wide * attention_wide, axis=1), 'head')]
    dot_general x18 -> x0, matrix products: 4.15 us -> none  [the longest x6 1.61 us: product(): return jnp.dot(left, right, preferred_element_type=jnp.float32)]
    unnamed x10 -> x0, local copies, waits for them, and re-layouts: 3.4 us -> none
    another operation x4 -> x0, other arithmetic: 2.4 us -> none
    slice x2 -> x0, local copies, waits for them, and re-layouts: 2.22 us -> none  [the longest x1 1.4 us: local(): blocks_on[0, slot_index] == 1]
  transfers between devices with their start and end apart: 8 -> 0, of which waited for: 2 -> 0; matrix products, arithmetic and copies ran while one was open for 6% -> 0% of each run, Pallas kernels for 0% -> 0%
where the time goes in v1:
time: 38.7 us; the launch traced here: 38.5 us
  Pallas kernels  37.8 us (98%)
  between operations  0.64 us (2%)
    pallas_call x1, Pallas kernels, local(): pl.pallas_call(functools.partial(kernel, heads, spacing, 8, peers), out_s...  37 us
    pallas_call x1, Pallas kernels, local(): pl.pallas_call(hand_on, out_shape=[block] * 4, in_specs=[vmem] * 4, out_s...  0.78 us

profile of v1, /device:TPU:6, one launch (start us, length us, event | category | flops | bytes accessed | tf_op | source)
XLA Modules:
  0.0 38.5 jit_solution(10610256245725599715)
XLA Ops:
  0.6 37.0 %attention.1 = (bf16[128,384]{1,0:T(8,128)(2,1)S(1)}, bf16[128,384]{1,0:T(8,128)(2,1)S(1)}, bf16[128,384]{1,0:T(8,128)(2,1)S(1)}, bf16[128,384]{1,0:T(8,128)(2,1)S(1)}) custom-call(bf16[128,384]{1,0:T(8,128)(2,1)} %q_hbm.1, bf16[128,384]{1,0:T(8,128)(2,1)} %k_hbm.1, bf16[128,384]{1,0:T(8,128)(2,1)} %v_hbm.1, bf16[128,384]{1,0:T(8,128)(2,1)} %do_hbm.1, ...), custom_call_target="tpu_custom_call" | custom-call | flops 505000000 | bytes 800000 | tf_op jit(solution)/shard_map/attention/pallas_call | solution.py:358
  37.7 0.8 %hand_on.1 = (bf16[128,384]{1,0:T(8,128)(2,1)}, bf16[128,384]{1,0:T(8,128)(2,1)}, bf16[128,384]{1,0:T(8,128)(2,1)}, bf16[128,384]{1,0:T(8,128)(2,1)}) custom-call(bf16[128,384]{1,0:T(8,128)(2,1)S(1)} %get-tuple-element.8.refs_0_, bf16[128,384]{1,0:T(8,128)(2,1)S(1)} %get-tuple-element.9.refs_1_, bf16[128,384]{1,0:T(8,128)(2,1)S(1)} %get-tuple-element.10.refs_2_, ...), custom_call_target="tpu_custom_call" | custom-call | tf_op jit(solution)/shard_map/hand_on/pallas_call | solution.py:388

commit v2 on v1

--- a/solution.py
+++ b/solution.py
@@ -68,6 +68,7 @@
     me = lax.axis_index("band")
     hd = lax.axis_index("head")
     z = me // spacing
+    core = lax.rem(me, 2)
     width = heads * D
     full_width = width * peers
     scaling = D ** (-0.5)
@@ -83,7 +84,7 @@
 
     barrier = pltpu.get_barrier_semaphore()
     expected = jnp.int32(peers - 1)
-    for d in (1, -1):
+    for d in COLUMN:
 
         @pl.when(inside(d))
         def _():
@@ -123,9 +124,9 @@
         sent.append((copy, condition))
         return copy
 
-    def first_step(src, dst_of, d):
+    def first_step(src, dst_of, d, also=True):
         copy = remote(src, dst_of(NEAR[d]), (me + d * spacing, hd), inside(d))
-        pl.when(inside(d))(copy.start)
+        pl.when(inside(d) & also)(copy.start)
         return copy
 
     def second_step(first, dst_of, d):
@@ -138,6 +139,14 @@
 
         return copy
 
+    def straight(src, dst_of, d):
+        copy = remote(src, dst_of(FAR[d]), (me + 2 * d * spacing, hd), inside(2 * d))
+        pl.when(inside(2 * d))(copy.start)
+        return copy
+
+    def near_arrived(first, d):
+        pl.when(inside(-d))(first.wait_recv)
+
     def arrived(second, d):
         pl.when(inside(-2 * d))(second.wait_recv)
 
@@ -149,7 +158,7 @@
 
     both = (1, -1)
     k1 = {(h, d): first_step(k_hbm.at[:, cols(h)], rows_of(kb, h), d) for h in range(heads) for d in both}
-    v1 = {(h, d): first_step(v_hbm.at[:, cols(h)], rows_of(vb, h), d) for h in range(heads) for d in both}
+    v1 = {(h, d): first_step(v_hbm.at[:, cols(h)], rows_of(vb, h), d, core != 1) for h in range(heads) for d in both}
 
     for d in both:
         for index, away in ((NEAR[d], -d), (FAR[d], -2 * d)):
@@ -187,11 +196,14 @@
             k2[h, d] = second_step(k1[h, d], rows_of(kb, h), d)
         for d in both:
             compute_scores(h, NEAR[d])
+    for h in range(heads):
+        for d in both:
+            pl.when(inside(d) & (core == 1))(v1[h, d].start)
     v2 = {}
     for h in range(heads):
         for d in both:
             v2[h, d] = second_step(v1[h, d], rows_of(vb, h), d)
-    q1 = {(h, d): first_step(q_hbm.at[:, cols(h)], rows_of(qb, h), d) for h in range(heads) for d in both}
+    q1 = {(h, d): first_step(q_hbm.at[:, cols(h)], rows_of(qb, h), d, core != 1) for h in range(heads) for d in both}
 
     lane = lax.broadcasted_iota(jnp.int32, (D, D), 1)
 
@@ -219,8 +231,12 @@
             probs[h, :, slot(i)] = weight.astype(BF16)
         peaks.append(peak)
         inverses.append(inverse_total)
+    for h in range(heads):
+        for d in both:
+            pl.when(inside(d) & (core == 1))(q1[h, d].start)
     st1[0] = as_rows(peaks + inverses + [-shift[offset] for offset in COLUMN])[0:16]
     s1 = {d: first_step(st1.at[0], tile_of(st1), d) for d in both}
+    s2 = {d: straight(st1.at[0], tile_of(st1), d) for d in both}
 
     near_rows = 3 * D
     partial = [nn(probs[h, :, 0:near_rows], vb[h, 0:near_rows]) for h in range(heads)]
@@ -241,7 +257,8 @@
         copy.start()
         exchanged.append(copy)
 
-    s2 = {d: second_step(s1[d], tile_of(st1), d) for d in both}
+    for d in both:
+        near_arrived(s1[d], d)
     q2 = {}
     for h in range(heads):
         for d in both:
@@ -285,6 +302,8 @@
     ]
     st2[0] = as_rows(deltas)[0:8]
     e1 = {d: first_step(st2.at[0], tile_of(st2), d) for d in both}
+    e2 = {d: straight(st2.at[0], tile_of(st2), d) for d in both}
+    a2 = {}
     for h in range(heads):
         out_ref[:, cols(h)] = (attn[h].astype(F32) * inverse_col * gain_ref[cols(h)][None, :]).astype(BF16)
 
@@ -312,11 +331,11 @@
             arrived(q2[h, d], d)
         for d in both:
             weights_back(h, FAR[d])
-    e2 = {d: second_step(e1[d], tile_of(st2), d) for d in both}
-    a2 = {}
     for h in range(heads):
         for d in both:
             a2[h, d] = second_step(a1[h, d], rows_of(ab, h), d)
+    for d in both:
+        near_arrived(e1[d], d)
     for h in range(heads):
         key_part, value_part = key_gradients(h, 1, 3)
         dk_acc[h] += key_part

time: 38.7 us -> 37.4 us (0.966)
  Pallas kernels: 37.8 us -> 36.6 us
    pallas_call x1, Pallas kernels: 37 us -> 35.8 us  [local(): pl.pallas_call(functools.partial(kernel, heads, spacing, 8, peers), out_s...]
where the time goes in v2:
time: 37.4 us; the launch traced here: 37.2 us
  Pallas kernels  36.6 us (98%)
  between operations  0.64 us (2%)
    pallas_call x1, Pallas kernels, local(): pl.pallas_call(functools.partial(kernel, heads, spacing, 8, peers), out_s...  35.8 us
    pallas_call x1, Pallas kernels, local(): pl.pallas_call(hand_on, out_shape=[block] * 4, in_specs=[vmem] * 4, out_s...  0.78 us

profile of v2, /device:TPU:6, one launch (start us, length us, event | category | flops | bytes accessed | tf_op | source)
XLA Modules:
  0.0 37.2 jit_solution(6797981424806005071)
XLA Ops:
  0.6 35.8 %attention.1 = (bf16[128,384]{1,0:T(8,128)(2,1)S(1)}, bf16[128,384]{1,0:T(8,128)(2,1)S(1)}, bf16[128,384]{1,0:T(8,128)(2,1)S(1)}, bf16[128,384]{1,0:T(8,128)(2,1)S(1)}) custom-call(bf16[128,384]{1,0:T(8,128)(2,1)} %q_hbm.1, bf16[128,384]{1,0:T(8,128)(2,1)} %k_hbm.1, bf16[128,384]{1,0:T(8,128)(2,1)} %v_hbm.1, bf16[128,384]{1,0:T(8,128)(2,1)} %do_hbm.1, ...), custom_call_target="tpu_custom_call" | custom-call | flops 505000000 | bytes 800000 | tf_op jit(solution)/shard_map/attention/pallas_call | solution.py:377
  36.4 0.8 %hand_on.1 = (bf16[128,384]{1,0:T(8,128)(2,1)}, bf16[128,384]{1,0:T(8,128)(2,1)}, bf16[128,384]{1,0:T(8,128)(2,1)}, bf16[128,384]{1,0:T(8,128)(2,1)}) custom-call(bf16[128,384]{1,0:T(8,128)(2,1)S(1)} %get-tuple-element.8.refs_0_, bf16[128,384]{1,0:T(8,128)(2,1)S(1)} %get-tuple-element.9.refs_1_, bf16[128,384]{1,0:T(8,128)(2,1)S(1)} %get-tuple-element.10.refs_2_, ...), custom_call_target="tpu_custom_call" | custom-call | tf_op jit(solution)/shard_map/hand_on/pallas_call | solution.py:407

commit v3 on v2

--- a/solution.py
+++ b/solution.py
@@ -51,6 +51,7 @@
     dob,
     gain_ref,
     on_ref,
+    grad,
     attn,
     score,
     probs,
@@ -205,6 +206,7 @@
             v2[h, d] = second_step(v1[h, d], rows_of(vb, h), d)
     q1 = {(h, d): first_step(q_hbm.at[:, cols(h)], rows_of(qb, h), d, core != 1) for h in range(heads) for d in both}
 
+    sums[0] = jnp.zeros(sums.shape[1:], F32)
     lane = lax.broadcasted_iota(jnp.int32, (D, D), 1)
 
     def as_rows(columns):
@@ -240,17 +242,20 @@
 
     near_rows = 3 * D
     partial = [nn(probs[h, :, 0:near_rows], vb[h, 0:near_rows]) for h in range(heads)]
-    sums_g, sums_a = [], []
+    for h in range(heads):
+        grad[h] = dob[h].astype(F32) * gain_ref[cols(h)][None, :]
+    sum_g = jnp.zeros((D, D), F32)
+    sum_a = jnp.zeros((D, D), F32)
     for h in range(heads):
         for d in both:
             arrived(v2[h, d], d)
         value = partial[h] + nn(probs[h, :, near_rows:], vb[h, near_rows:])
         attn[h] = value.astype(BF16)
         wide = attn[h].astype(F32)
-        gradient = dob[h].astype(F32) * gain_ref[cols(h)][None, :]
-        sums_g.append(jnp.sum(gradient * wide, axis=1, keepdims=True))
-        sums_a.append(jnp.sum(wide * wide, axis=1, keepdims=True))
-    sums[0] = as_rows([functools.reduce(jnp.add, sums_g), functools.reduce(jnp.add, sums_a)])[0:8]
+        sum_g += grad[h] * wide
+        sum_a += wide * wide
+    sums[0, 0:1] = jnp.sum(sum_g.T, axis=0, keepdims=True)
+    sums[0, 1:2] = jnp.sum(sum_a.T, axis=0, keepdims=True)
     exchanged = []
     for p in range(1, peers):
         copy = remote(sums.at[0], sums.at[p], (me, lax.rem(hd + p, peers)), True)
@@ -292,7 +297,7 @@
     coefficient_col = columns[:, 1:2]
     a1 = {}
     for h in range(heads):
-        gradient = dob[h].astype(F32) * gain_ref[cols(h)][None, :]
+        gradient = grad[h]
         wide = attn[h].astype(F32)
         ab[h, slot(0)] = (inverse_col * gradient - wide * coefficient_col).astype(BF16)
         for d in both:
@@ -384,6 +389,7 @@
             pltpu.VMEM((heads, D, D), BF16),
             pltpu.VMEM((width,), F32),
             pltpu.SMEM((1, 4), jnp.int32),
+            pltpu.VMEM((heads, D, D), F32),
             pltpu.VMEM((heads, D, D), BF16),
             pltpu.VMEM((heads, D, 5 * D), F32),
             pltpu.VMEM((heads, D, 5 * D), BF16),

time: 37.4 us -> 37.6 us (level)
  no operation moved by 1% of the time
where the time goes in v3:
time: 37.6 us; the launch traced here: 37.2 us
  Pallas kernels  36.5 us (97%)
  between operations  0.64 us (2%)
    pallas_call x1, Pallas kernels, local(): pl.pallas_call(functools.partial(kernel, heads, spacing, 8, peers), out_s...  35.8 us
    pallas_call x1, Pallas kernels, local(): pl.pallas_call(hand_on, out_shape=[block] * 4, in_specs=[vmem] * 4, out_s...  0.78 us

profile of v3, /device:TPU:6, one launch (start us, length us, event | category | flops | bytes accessed | tf_op | source)
XLA Modules:
  0.0 37.2 jit_solution(4532907498218363327)
XLA Ops:
  0.6 35.8 %attention.1 = (bf16[128,384]{1,0:T(8,128)(2,1)S(1)}, bf16[128,384]{1,0:T(8,128)(2,1)S(1)}, bf16[128,384]{1,0:T(8,128)(2,1)S(1)}, bf16[128,384]{1,0:T(8,128)(2,1)S(1)}) custom-call(bf16[128,384]{1,0:T(8,128)(2,1)} %q_hbm.1, bf16[128,384]{1,0:T(8,128)(2,1)} %k_hbm.1, bf16[128,384]{1,0:T(8,128)(2,1)} %v_hbm.1, bf16[128,384]{1,0:T(8,128)(2,1)} %do_hbm.1, ...), custom_call_target="tpu_custom_call" | custom-call | flops 505000000 | bytes 800000 | tf_op jit(solution)/shard_map/attention/pallas_call | solution.py:382
  36.4 0.8 %hand_on.1 = (bf16[128,384]{1,0:T(8,128)(2,1)}, bf16[128,384]{1,0:T(8,128)(2,1)}, bf16[128,384]{1,0:T(8,128)(2,1)}, bf16[128,384]{1,0:T(8,128)(2,1)}) custom-call(bf16[128,384]{1,0:T(8,128)(2,1)S(1)} %get-tuple-element.8.refs_0_, bf16[128,384]{1,0:T(8,128)(2,1)S(1)} %get-tuple-element.9.refs_1_, bf16[128,384]{1,0:T(8,128)(2,1)S(1)} %get-tuple-element.10.refs_2_, ...), custom_call_target="tpu_custom_call" | custom-call | tf_op jit(solution)/shard_map/hand_on/pallas_call | solution.py:413

commit v4 on v2

--- a/solution.py
+++ b/solution.py
@@ -303,7 +303,7 @@
     st2[0] = as_rows(deltas)[0:8]
     e1 = {d: first_step(st2.at[0], tile_of(st2), d) for d in both}
     e2 = {d: straight(st2.at[0], tile_of(st2), d) for d in both}
-    a2 = {}
+    a2 = {(heads - 1, d): straight(ab.at[heads - 1, slot(0)], rows_of(ab, heads - 1), d) for d in both}
     for h in range(heads):
         out_ref[:, cols(h)] = (attn[h].astype(F32) * inverse_col * gain_ref[cols(h)][None, :]).astype(BF16)
 
@@ -331,10 +331,11 @@
             arrived(q2[h, d], d)
         for d in both:
             weights_back(h, FAR[d])
-    for h in range(heads):
+    for h in range(heads - 1):
         for d in both:
             a2[h, d] = second_step(a1[h, d], rows_of(ab, h), d)
     for d in both:
+        near_arrived(a1[heads - 1, d], d)
         near_arrived(e1[d], d)
     for h in range(heads):
         key_part, value_part = key_gradients(h, 1, 3)

time: 37.4 us -> 37.9 us (1.013)
  the two profiles are of different devices: /device:TPU:6 before, /device:TPU:1 now
where the time goes in v4:
time: 37.9 us; the launch traced here: 37.7 us
  Pallas kernels  37 us (98%)
  between operations  0.64 us (2%)
    pallas_call x1, Pallas kernels, local(): pl.pallas_call(functools.partial(kernel, heads, spacing, 8, peers), out_s...  36.3 us
    pallas_call x1, Pallas kernels, local(): pl.pallas_call(hand_on, out_shape=[block] * 4, in_specs=[vmem] * 4, out_s...  0.78 us

profile of v4, /device:TPU:1, one launch (start us, length us, event | category | flops | bytes accessed | tf_op | source)
XLA Modules:
  0.0 37.7 jit_solution(1745820951702543446)
XLA Ops:
  0.6 36.3 %attention.1 = (bf16[128,384]{1,0:T(8,128)(2,1)S(1)}, bf16[128,384]{1,0:T(8,128)(2,1)S(1)}, bf16[128,384]{1,0:T(8,128)(2,1)S(1)}, bf16[128,384]{1,0:T(8,128)(2,1)S(1)}) custom-call(bf16[128,384]{1,0:T(8,128)(2,1)} %q_hbm.1, bf16[128,384]{1,0:T(8,128)(2,1)} %k_hbm.1, bf16[128,384]{1,0:T(8,128)(2,1)} %v_hbm.1, bf16[128,384]{1,0:T(8,128)(2,1)} %do_hbm.1, ...), custom_call_target="tpu_custom_call" | custom-call | flops 505000000 | bytes 800000 | tf_op jit(solution)/shard_map/attention/pallas_call | solution.py:378
  36.9 0.8 %hand_on.1 = (bf16[128,384]{1,0:T(8,128)(2,1)}, bf16[128,384]{1,0:T(8,128)(2,1)}, bf16[128,384]{1,0:T(8,128)(2,1)}, bf16[128,384]{1,0:T(8,128)(2,1)}) custom-call(bf16[128,384]{1,0:T(8,128)(2,1)S(1)} %get-tuple-element.8.refs_0_, bf16[128,384]{1,0:T(8,128)(2,1)S(1)} %get-tuple-element.9.refs_1_, bf16[128,384]{1,0:T(8,128)(2,1)S(1)} %get-tuple-element.10.refs_2_, ...), custom_call_target="tpu_custom_call" | custom-call | tf_op jit(solution)/shard_map/hand_on/pallas_call | solution.py:408

commit v5 on v3

--- a/solution.py
+++ b/solution.py
@@ -233,14 +233,14 @@
             probs[h, :, slot(i)] = weight.astype(BF16)
         peaks.append(peak)
         inverses.append(inverse_total)
-    for h in range(heads):
-        for d in both:
-            pl.when(inside(d) & (core == 1))(q1[h, d].start)
     st1[0] = as_rows(peaks + inverses + [-shift[offset] for offset in COLUMN])[0:16]
     s1 = {d: first_step(st1.at[0], tile_of(st1), d) for d in both}
     s2 = {d: straight(st1.at[0], tile_of(st1), d) for d in both}
 
     near_rows = 3 * D
+    for h in range(heads):
+        for d in both:
+            pl.when(inside(d) & (core == 1))(q1[h, d].start)
     partial = [nn(probs[h, :, 0:near_rows], vb[h, 0:near_rows]) for h in range(heads)]
     for h in range(heads):
         grad[h] = dob[h].astype(F32) * gain_ref[cols(h)][None, :]

time: 37.6 us -> 37.4 us (level)
  no operation moved by 1% of the time
where the time goes in v5:
time: 37.4 us; the launch traced here: 37.2 us
  Pallas kernels  36.5 us (98%)
  between operations  0.64 us (2%)
    pallas_call x1, Pallas kernels, local(): pl.pallas_call(functools.partial(kernel, heads, spacing, 8, peers), out_s...  35.8 us
    pallas_call x1, Pallas kernels, local(): pl.pallas_call(hand_on, out_shape=[block] * 4, in_specs=[vmem] * 4, out_s...  0.78 us

profile of v5, /device:TPU:6, one launch (start us, length us, event | category | flops | bytes accessed | tf_op | source)
XLA Modules:
  0.0 37.2 jit_solution(17721964921078001739)
XLA Ops:
  0.6 35.8 %attention.1 = (bf16[128,384]{1,0:T(8,128)(2,1)S(1)}, bf16[128,384]{1,0:T(8,128)(2,1)S(1)}, bf16[128,384]{1,0:T(8,128)(2,1)S(1)}, bf16[128,384]{1,0:T(8,128)(2,1)S(1)}) custom-call(bf16[128,384]{1,0:T(8,128)(2,1)} %q_hbm.1, bf16[128,384]{1,0:T(8,128)(2,1)} %k_hbm.1, bf16[128,384]{1,0:T(8,128)(2,1)} %v_hbm.1, bf16[128,384]{1,0:T(8,128)(2,1)} %do_hbm.1, ...), custom_call_target="tpu_custom_call" | custom-call | flops 505000000 | bytes 800000 | tf_op jit(solution)/shard_map/attention/pallas_call | solution.py:382
  36.4 0.8 %hand_on.1 = (bf16[128,384]{1,0:T(8,128)(2,1)}, bf16[128,384]{1,0:T(8,128)(2,1)}, bf16[128,384]{1,0:T(8,128)(2,1)}, bf16[128,384]{1,0:T(8,128)(2,1)}) custom-call(bf16[128,384]{1,0:T(8,128)(2,1)S(1)} %get-tuple-element.8.refs_0_, bf16[128,384]{1,0:T(8,128)(2,1)S(1)} %get-tuple-element.9.refs_1_, bf16[128,384]{1,0:T(8,128)(2,1)S(1)} %get-tuple-element.10.refs_2_, ...), custom_call_target="tpu_custom_call" | custom-call | tf_op jit(solution)/shard_map/hand_on/pallas_call | solution.py:413
